TPU v7x, 256 devices: a whole 4x4x8 slice. The times are simulated.
256 devices in a mesh: space: 32 (over z_lo, y, core), fac: 8 (over z_hi, x).
Axes of the slice: x: 4, y: 4, z: 8 (z_hi: 2, z_lo: 4; z = z_hi * 4 + z_lo), core: 2. Of those that a mesh axis runs over, the one named last changes fastest.
Arguments:
- activations: bfloat16 [8, 64, 16, 16, 128], P('fac', 'space'), may hold values from -60 to 60
- out_grad: bfloat16 [8, 64, 16, 16, 128], P('fac', 'space'), may hold values from -60 to 60
- kernel: bfloat16 [27, 128, 128], replicated, may hold values from -0.109375 to 0.109375
Outputs:
- in_grad: bfloat16 [8, 64, 16, 16, 128], P('fac', 'space')
- update: float32 [27, 128, 128], P(None, 'fac')
All inputs are finite; a program needn't handle non-finite values.
Results may differ from a plain program's by a relative error of at most 0.0014.
Values may be sent and summed in bfloat16 or wider, within the bound.
No kernel may reach another device: no remote copies, remote signals or barrier semaphores. Data moves between devices by JAX's collectives and lax.ppermute only.
A program may use at most 128 MiB of HBM per device.

v0:
```python
import math
import jax
import jax.numpy as jnp
from jax import lax
from jax.sharding import PartitionSpec as P

damping = 0.1
clip_rate = 0.05


def with_halo(cells, sides, width):
    for axis, dim in sides:
        count = lax.axis_size(axis)
        ends = count - 1
        head = lax.slice_in_dim(cells, 0, width, axis=dim)
        tail = lax.slice_in_dim(cells, cells.shape[dim] - width, cells.shape[dim], axis=dim)
        cells = jnp.concatenate(
            [
                lax.ppermute(tail, axis, [(i, (i + 1) % count) for i in range(ends)]),
                cells,
                lax.ppermute(head, axis, [((i + 1) % count, i) for i in range(ends)]),
            ],
            axis=dim,
        )
    return cells


def offsets():
    return [(a, b, c) for a in (-1, 0, 1) for b in (-1, 0, 1) for c in (-1, 0, 1)]


def window(padded, shift, extent):
    return padded[
        1 + shift[0] : 1 + shift[0] + extent[0],
        1 + shift[1] : 1 + shift[1] + extent[1],
        1 + shift[2] : 1 + shift[2] + extent[2],
    ]


def local_stats(padded_in, rows_cot, extent, groups):
    cells = rows_cot.shape[0]
    width = padded_in.shape[-1] // groups
    gram_list = []
    grad_list = []
    for block_index in range(groups):
        lower = block_index * width
        pieces = [
            window(padded_in, shift, extent)[..., lower : lower + width].reshape(cells, width)
            for shift in offsets()
        ]
        patch = jnp.concatenate(pieces, axis=1)
        gram_list.append(jnp.dot(patch.T, patch, preferred_element_type=jnp.float32))
        grad_list.append(jnp.dot(patch.T, rows_cot, preferred_element_type=jnp.float32))
    grads = jnp.stack(grad_list)
    return (jnp.stack(gram_list), grads)


def on_device(activations, out_grad, kernel):
    inputs = activations[0]
    cotangent = out_grad[0]
    size_x, size_y, size_z, channels = inputs.shape
    extent = (size_x, size_y, size_z)
    cells = size_x * size_y * size_z
    groups = lax.axis_size("fac")
    width = channels // groups
    stacked = jnp.concatenate([inputs, cotangent], axis=3)
    rimmed = with_halo(stacked, (("space", 0),), 1)
    padded = jnp.pad(rimmed, ((0, 0), (1, 1), (1, 1), (0, 0)))
    padded_in = padded[..., :channels]
    padded_cot = padded[..., channels:]
    rows_cot = cotangent.reshape(cells, channels)
    cot_gram = jnp.dot(rows_cot.T, rows_cot, preferred_element_type=jnp.float32)
    in_grad = jnp.zeros((cells, channels), jnp.float32)
    for tap_index, shift in enumerate(offsets()):
        back = (-shift[0], -shift[1], -shift[2])
        rows = window(padded_cot, back, extent).reshape(cells, channels)
        in_grad = in_grad + jnp.dot(rows, kernel[tap_index].T, preferred_element_type=jnp.float32)
    in_grad = in_grad.astype(jnp.bfloat16).reshape(activations.shape)
    cot_total = lax.psum(cot_gram, ("space", "fac"))
    grams, grads = local_stats(padded_in, rows_cot, extent, groups)
    summed = lax.psum((grams, grads), "space")
    owned = (
        lax.psum_scatter(summed[0], "fac", scatter_dimension=0, tiled=True),
        lax.psum_scatter(summed[1], "fac", scatter_dimension=0, tiled=True),
    )
    gram_block = owned[0][0]
    grad_block = owned[1][0]
    count = float(cells * lax.axis_size("space") * groups)
    order = gram_block.shape[0]
    right_mat = cot_total / count + damping * jnp.eye(channels, dtype=jnp.float32)
    right_chol = jnp.linalg.cholesky(right_mat)
    left_mat = gram_block / count + damping * jnp.eye(order, dtype=jnp.float32)
    left_chol = jnp.linalg.cholesky(left_mat)
    scaled = grad_block / math.sqrt(count)
    half = jax.scipy.linalg.cho_solve((left_chol, True), scaled)
    raw = jax.scipy.linalg.cho_solve((right_chol, True), half.T).T
    total = lax.psum(jnp.sum(raw * scaled), "fac")
    factor = jnp.sqrt(clip_rate * kernel.size / total)
    update = raw.reshape(27, width, channels) * factor
    return (in_grad, update)


def solution(mesh):
    placed = (P("fac", "space", None, None, None), P("fac", "space", None, None, None), P())
    return jax.shard_map(
        on_device,
        mesh=mesh,
        in_specs=placed,
        out_specs=(P("fac", "space", None, None, None), P(None, "fac", None)),
        check_vma=False,
    )
```

profile of v0, /device:TPU:0, one launch (start us, length us, event | category | flops | bytes accessed | tf_op | source)
XLA Modules:
  0.0 795.9 jit_solution(12100450884241944340)
XLA Ops:
  8.1 1.9 convolution_bitcast_fusion.16
  16.7 1.6 fusion.150
  18.4 1.7 fusion.154
  20.1 2.2 fusion.152
  22.3 2.3 fusion.148
  24.6 2.3 fusion.149
  26.9 2.2 fusion.146
  29.1 2.2 fusion.153
  31.3 2.3 fusion.147
  33.6 2.2 fusion.151
  35.8 2.2 fusion.145
  38.1 1.9 fusion.158
  40.0 3.3 concatenate.80
  44.4 3.4 concatenate.81
  48.8 3.3 concatenate.82
  53.1 3.4 concatenate.83
  57.4 4.2 concatenate.84
  61.7 2.1 fusion.14
  63.7 4.2 concatenate.85
  68.0 2.1 fusion.13
  70.0 4.2 concatenate.86
  74.3 2.1 fusion.12
  76.3 4.2 concatenate.87
  80.6 2.0 fusion.11
  82.7 1.4 fusion.10
  84.0 1.4 fusion.9
  86.8 1.4 fusion.7
  90.8 1.4 fusion.4
  94.5 214.7 %all-reduce.8.cloned.1.call-done = f32[128,128]{1,0:T(8,128)} async-done(((f32[128,128]{1,0:T(8,128)}), f32[128,128]{1,0:T(8,128)}) %all-reduce.8.cloned.1.call-update) | async-done | bytes 65552 | tf_op jit(solution)/shard_map/psum | solution.py:79
  311.0 11.7 %cholesky.100 = f32[128,128]{1,0:T(8,128)S(1)} custom-call(f32[128,128]{1,0:T(8,128)S(1)} %fusion.73), custom_call_target="Cholesky" | custom-call | tf_op jit(solution)/shard_map/jit(cholesky)/cholesky | solution.py:91
  324.0 10.4 %custom-call.44 = f32[1,128,128]{1,2,0:T(8,128)} custom-call(f32[1,128,128]{2,1,0:T(8,128)S(1)} %fusion.62), custom_call_target="InvertDiagBlocksLowerTriangular" | custom-call | tf_op jit(solution)/shard_map/jit(_cho_solve)/triangular_solve | solution.py:96
  334.5 1.6 slice.1801
  340.9 9.6 %reduce-scatter.3.cloned.1.call-done = f32[1,432,432]{2,1,0:T(8,128)} async-done(((f32[8,432,432]{2,1,0:T(8,128)}), f32[1,432,432]{2,1,0:T(8,128)}) %reduce-scatter.3.cloned.1.call-update) | async-done | bytes 746512 | tf_op jit(solution)/shard_map/reduce_scatter | solution.py:83
  352.1 268.3 %all-reduce.10.cloned.1.call-done = (f32[1,432,432]{2,1,0:T(8,128)}, f32[1,432,128]{2,1,0:T(8,128)}) async-done(((f32[1,432,432]{2,1,0:T(8,128)}, f32[1,432,128]{2,1,0:T(8,128)}), (f32[1,432,432]{2,1,0:T(8,128)}, f32[1,432,128]{2,1,0:T(8,128)})) %all-reduce.10.cloned.1.call-update) | async-done | bytes 967696 | tf_op jit(solution)/shard_map/psum | solution.py:81
  621.4 1.4 bitcast_add_fusion.1
  623.3 12.1 %cholesky.109 = f32[128,128]{1,0:T(8,128)S(1)} custom-call(f32[128,128]{1,0:T(8,128)S(1)} %cholesky.264), custom_call_target="Cholesky" | custom-call | tf_op jit(solution)/shard_map/jit(cholesky)/cholesky | solution.py:93
  636.2 9.8 %custom-call.45 = f32[1,128,128]{1,2,0:T(8,128)S(1)} custom-call(f32[1,128,128]{2,1,0:T(8,128)S(1)} %get-tuple-element.273), custom_call_target="InvertDiagBlocksLowerTriangular" | custom-call | tf_op jit(solution)/shard_map/jit(cholesky)/cholesky | solution.py:93
  648.6 11.7 %cholesky.212 = f32[128,128]{1,0:T(8,128)S(1)} custom-call(f32[128,128]{1,0:T(8,128)S(1)} %cholesky.268), custom_call_target="Cholesky" | custom-call | tf_op jit(solution)/shard_map/jit(cholesky)/cholesky | solution.py:93
  661.0 9.8 %custom-call.46 = f32[1,128,128]{1,2,0:T(8,128)S(1)} custom-call(f32[1,128,128]{2,1,0:T(8,128)S(1)} %get-tuple-element.270), custom_call_target="InvertDiagBlocksLowerTriangular" | custom-call | tf_op jit(solution)/shard_map/jit(cholesky)/cholesky | solution.py:93
  672.3 11.9 %cholesky.233 = f32[128,128]{1,0:T(8,128)S(1)} custom-call(f32[128,128]{1,0:T(8,128)S(1)} %cholesky.273), custom_call_target="Cholesky" | custom-call | tf_op jit(solution)/shard_map/jit(cholesky)/cholesky | solution.py:93
  684.8 9.8 %custom-call.47 = f32[1,128,128]{1,2,0:T(8,128)S(1)} custom-call(f32[1,128,128]{2,1,0:T(8,128)S(1)} %get-tuple-element.267), custom_call_target="InvertDiagBlocksLowerTriangular" | custom-call | tf_op jit(solution)/shard_map/jit(cholesky)/cholesky | solution.py:93
  695.8 4.4 cholesky.253
  703.5 6.1 while.1
  704.2 1.4 bitcast_dynamic-update-slice_fusion.2
  706.2 1.4 bitcast_dynamic-update-slice_fusion.2
  708.2 1.4 bitcast_dynamic-update-slice_fusion.2
  709.8 39.3 %custom-call.48 = f32[4,128,128]{1,2,0:T(8,128)S(1)} custom-call(f32[4,128,128]{2,1,0:T(8,128)S(1)} %pad_maximum_fusion.1), custom_call_target="InvertDiagBlocksLowerTriangular" | custom-call | tf_op jit(solution)/shard_map/jit(_cho_solve)/triangular_solve | solution.py:95
  754.6 32.0 %psum.31 = f32[]{:T(128)} all-reduce(f32[]{:T(128)} %get-tuple-element.278), channel_id=1, replica_groups=mesh['space'=32,'fac'=8] {'fac'}, use_global_device_ids=true, to_apply=%region_16.17 | all-reduce | flops 1 | bytes 8 | tf_op jit(solution)/shard_map/psum | solution.py:97
  (147 shorter events, 44.4 us)
Async XLA Ops:
  8.0 7.6 copy-start
  8.0 5.6 copy-start.1
  8.0 301.1 %all-reduce.8.cloned.1.call-start = ((), (), s32[]{:S(2)}) async-start(), calls=%async_computation.2 | async-start | bytes 131072 | tf_op jit(solution)/shard_map/psum | solution.py:79
  9.9 330.9 %reduce-scatter.5.cloned.1.call-start = ((), (), s32[]{:S(2)}) async-start(), calls=%async_computation.4 | async-start | bytes 1990656 | tf_op jit(solution)/shard_map/reduce_scatter | solution.py:84
  11.0 3.8 collective-permute-start
  12.3 3.3 collective-permute-start.1
  38.1 1.9 copy-start.6
  44.4 4.4 copy-start.11
  82.6 267.9 %reduce-scatter.3.cloned.1.call-start = ((), (), s32[]{:S(2)}) async-start(), calls=%async_computation.3 | async-start | bytes 7962624 | tf_op jit(solution)/shard_map/reduce_scatter | solution.py:83
  85.4 2.7 copy-start.2
  86.8 2.7 copy-start.3
  88.1 2.7 copy-start.4
  89.5 2.7 copy-start.5
  93.6 242.6 %copy-start.10 = (bf16[27,128,128]{2,1,0:T(8,128)(2,1)S(1)}, bf16[27,128,128]{2,1,0:T(8,128)(2,1)}, u32[]{:S(2)}) copy-start(bf16[27,128,128]{2,1,0:T(8,128)(2,1)} %param.5) | copy-start | bytes 2654212
  93.6 526.9 %all-reduce.10.cloned.1.call-start = ((), (), s32[]{:S(2)}) async-start(), calls=%async_computation.5 | async-start | bytes 2211840 | tf_op jit(solution)/shard_map/psum | solution.py:81
  340.0 10.5 %copy-start.12 = (bf16[2,16,16,128]{3,2,1,0:T(8,128)(2,1)S(1)}, bf16[2,16,16,128]{3,2,1,0:T(8,128)(2,1)}, u32[]{:S(2)}) copy-start(bf16[2,16,16,128]{3,2,1,0:T(8,128)(2,1)} %slice.1801) | copy-start | bytes 393220
  621.4 1.7 copy-start.7
  623.3 12.9 %copy-start.8 = (f32[432,432]{1,0:T(8,128)}, f32[432,432]{1,0:T(8,128)S(1)}, u32[]{:S(2)}) copy-start(f32[432,432]{1,0:T(8,128)S(1)} %fusion.25) | copy-start | bytes 2239492
  648.5 55.0 %copy-start.15 = (f32[3,128,128]{2,1,0:T(8,128)S(1)}, f32[3,128,128]{2,1,0:T(8,128)}, u32[]{:S(2)}) copy-start(f32[3,128,128]{2,1,0:T(8,128)} %custom-call.51) | copy-start | bytes 589828
  672.2 37.4 %copy-start.13 = (f32[128,80]{1,0:T(8,128)S(1)}, f32[128,80]{1,0:T(8,128)}, u32[]{:S(2)}) copy-start(f32[128,80]{1,0:T(8,128)} %pad_convert_fusion) | copy-start | bytes 122884
  709.7 43.3 %copy-start.14 = (f32[1,128,128]{1,2,0:T(8,128)S(1)}, f32[1,128,128]{1,2,0:T(8,128)}, u32[]{:S(2)}) copy-start(f32[1,128,128]{1,2,0:T(8,128)} %custom-call.44) | copy-start | bytes 196612
  749.4 4.1 copy-start.9
Sparse Core Ops, SparseCore 0:
  14.4 294.7 all-reduce.7
Sparse Core Ops, SparseCore 1:
  82.7 99.6 reduce-scatter.4
  186.6 163.9 reduce-scatter.2
  353.3 267.1 all-reduce.9
where the time goes:
time: 806 us; the launch traced here: 796 us
  waiting for transfers between devices  494 us (61%)
  other arithmetic  142 us (18%)
  local copies, waits for them, and re-layouts  64 us (8%)
  matrix products  41.1 us (5%)
  blocking collectives  32 us (4%)
  between operations  19.9 us (2%)
    psum x1, waiting for transfers between devices, on_device(): summed = lax.psum((grams, grads), 'space')  268 us
    psum x1, waiting for transfers between devices, on_device(): cot_total = lax.psum(cot_gram, ('space', 'fac'))  215 us
    another operation x15, other arithmetic, on_device(): left_chol = jnp.linalg.cholesky(left_mat)  72.3 us
    another operation x7, other arithmetic, on_device(): half = jax.scipy.linalg.cho_solve((left_chol, True), scaled)  40.2 us
    psum x1, blocking collectives, on_device(): total = lax.psum(jnp.sum(raw * scaled), 'fac')  32 us
    concatenate x8, local copies, waits for them, and re-layouts, local_stats(): patch = jnp.concatenate(pieces, axis=1)  30.3 us
    slice x13, local copies, waits for them, and re-layouts, local_stats(): window(padded_in, shift, extent)[..., lower:lower + width]  25.1 us
  transfers between devices with their start and end apart: 6, of which 4 were waited for; matrix products, arithmetic and copies ran while one was open for 14% of the time, Pallas kernels for 0%

commit v1 on v0

--- a/solution.py
+++ b/solution.py
@@ -76,7 +76,7 @@
         rows = window(padded_cot, back, extent).reshape(cells, channels)
         in_grad = in_grad + jnp.dot(rows, kernel[tap_index].T, preferred_element_type=jnp.float32)
     in_grad = in_grad.astype(jnp.bfloat16).reshape(activations.shape)
-    cot_total = lax.psum(cot_gram, ("space", "fac"))
+    cot_total = jnp.sum(lax.all_gather(cot_gram, ("space", "fac")), axis=0)
     grams, grads = local_stats(padded_in, rows_cot, extent, groups)
     summed = lax.psum((grams, grads), "space")
     owned = (

time: 806 us -> 1170 us (1.45)
  waiting for transfers between devices: 494 us -> 854 us
    all_gather x0 -> x1, waiting for transfers between devices: none -> 336 us  [on_device(): cot_total = jnp.sum(lax.all_gather(cot_gram, ('space', 'fac')), axis=0)]
    psum x1 -> x0, waiting for transfers between devices: 215 us -> none  [on_device(): cot_total = lax.psum(cot_gram, ('space', 'fac'))]
    reduce_scatter x1, waiting for transfers between devices: 9.63 us -> 168 us  [on_device(): lax.psum_scatter(summed[0], 'fac', scatter_dimension=0, tiled=True)]
    reduce_scatter x1, waiting for transfers between devices: 0.03 us -> 87.7 us  [on_device(): lax.psum_scatter(summed[1], 'fac', scatter_dimension=0, tiled=True)]
  transfers between devices with their start and end apart: 6 -> 6, of which waited for: 4 -> 4; matrix products, arithmetic and copies ran while one was open for 14% -> 13% of each run, Pallas kernels for 0% -> 0%
where the time goes in v1:
time: 1170 us; the launch traced here: 1160 us
  waiting for transfers between devices  854 us (73%)
  other arithmetic  145 us (12%)
  local copies, waits for them, and re-layouts  64.9 us (6%)
  matrix products  40.1 us (3%)
  blocking collectives  28.6 us (2%)
  between operations  19.2 us (2%)
    all_gather x1, waiting for transfers between devices, on_device(): cot_total = jnp.sum(lax.all_gather(cot_gram, ('space', 'fac')), axis=0)  336 us
    psum x1, waiting for transfers between devices, on_device(): summed = lax.psum((grams, grads), 'space')  262 us
    reduce_scatter x1, waiting for transfers between devices, on_device(): lax.psum_scatter(summed[0], 'fac', scatter_dimension=0, tiled=True)  168 us
    reduce_scatter x1, waiting for transfers between devices, on_device(): lax.psum_scatter(summed[1], 'fac', scatter_dimension=0, tiled=True)  87.7 us
    another operation x15, other arithmetic, on_device(): left_chol = jnp.linalg.cholesky(left_mat)  72 us
    another operation x7, other arithmetic, on_device(): half = jax.scipy.linalg.cho_solve((left_chol, True), scaled)  40.2 us
    concatenate x8, local copies, waits for them, and re-layouts, local_stats(): patch = jnp.concatenate(pieces, axis=1)  30.2 us
    psum x1, blocking collectives, on_device(): total = lax.psum(jnp.sum(raw * scaled), 'fac')  28.6 us
  transfers between devices with their start and end apart: 6, of which 4 were waited for; matrix products, arithmetic and copies ran while one was open for 13% of the time, Pallas kernels for 0%

profile of v1, /device:TPU:0, one launch (start us, length us, event | category | flops | bytes accessed | tf_op | source)
XLA Modules:
  0.0 1155.4 jit_solution(13497837302150111990)
XLA Ops:
  11.7 2.7 fusion.161
  15.6 1.7 fusion.151
  17.3 1.8 fusion.155
  19.1 2.2 fusion.153
  21.3 2.3 fusion.149
  23.5 2.3 fusion.150
  25.8 2.2 fusion.147
  28.1 2.3 fusion.154
  30.3 2.2 fusion.148
  32.5 2.2 fusion.152
  34.8 2.2 fusion.146
  37.1 1.9 fusion.159
  39.0 3.3 concatenate.80
  43.3 3.4 concatenate.81
  47.7 3.3 concatenate.82
  52.1 3.4 concatenate.83
  56.4 4.2 concatenate.84
  60.6 2.0 fusion.14
  62.7 4.2 concatenate.85
  66.9 2.0 fusion.13
  68.9 4.2 concatenate.86
  73.2 2.0 fusion.12
  75.2 4.2 concatenate.87
  79.4 2.0 fusion.11
  81.5 1.4 fusion.10
  82.9 1.4 fusion.9
  85.6 1.4 fusion.7
  89.7 1.4 fusion.4
  92.5 87.7 %reduce-scatter.5.cloned.1.call-done = f32[1,432,128]{2,1,0:T(8,128)} async-done(((f32[8,432,128]{2,1,0:T(8,128)}), f32[1,432,128]{2,1,0:T(8,128)}) %reduce-scatter.5.cloned.1.call-update) | async-done | bytes 221200 | tf_op jit(solution)/shard_map/reduce_scatter | solution.py:84
  180.1 168.3 %reduce-scatter.3.cloned.1.call-done = f32[1,432,432]{2,1,0:T(8,128)} async-done(((f32[8,432,432]{2,1,0:T(8,128)}), f32[1,432,432]{2,1,0:T(8,128)}) %reduce-scatter.3.cloned.1.call-update) | async-done | bytes 746512 | tf_op jit(solution)/shard_map/reduce_scatter | solution.py:83
  357.6 262.1 %all-reduce.7.cloned.1.call-done = (f32[1,432,432]{2,1,0:T(8,128)}, f32[1,432,128]{2,1,0:T(8,128)}) async-done(((f32[1,432,432]{2,1,0:T(8,128)}, f32[1,432,128]{2,1,0:T(8,128)}), (f32[1,432,432]{2,1,0:T(8,128)}, f32[1,432,128]{2,1,0:T(8,128)})) %all-reduce.7.cloned.1.call-update) | async-done | bytes 967696 | tf_op jit(solution)/shard_map/psum | solution.py:81
  621.7 11.7 %cholesky.109 = f32[128,128]{1,0:T(8,128)S(1)} custom-call(f32[128,128]{1,0:T(8,128)S(1)} %cholesky.264), custom_call_target="Cholesky" | custom-call | tf_op jit(solution)/shard_map/jit(cholesky)/cholesky | solution.py:93
  633.4 9.8 custom-call.45
  645.8 12.1 %cholesky.212 = f32[128,128]{1,0:T(8,128)S(1)} custom-call(f32[128,128]{1,0:T(8,128)S(1)} %cholesky.268), custom_call_target="Cholesky" | custom-call | tf_op jit(solution)/shard_map/jit(cholesky)/cholesky | solution.py:93
  657.9 9.8 custom-call.46
  669.2 11.7 %cholesky.233 = f32[128,128]{1,0:T(8,128)S(1)} custom-call(f32[128,128]{1,0:T(8,128)S(1)} %cholesky.273), custom_call_target="Cholesky" | custom-call | tf_op jit(solution)/shard_map/jit(cholesky)/cholesky | solution.py:93
  681.0 9.8 custom-call.47
  692.0 4.4 cholesky.253
  701.5 6.1 while.1
  702.3 1.4 bitcast_dynamic-update-slice_fusion.2
  704.2 1.4 bitcast_dynamic-update-slice_fusion.2
  706.2 1.4 bitcast_dynamic-update-slice_fusion.2
  707.6 39.3 %custom-call.48 = f32[4,128,128]{1,2,0:T(8,128)S(1)} custom-call(f32[4,128,128]{2,1,0:T(8,128)S(1)} %pad_maximum_fusion.1), custom_call_target="InvertDiagBlocksLowerTriangular" | custom-call | tf_op jit(solution)/shard_map/jit(_cho_solve)/triangular_solve | solution.py:95
  750.9 335.8 %all-gather.3.cloned.1.call-done = f32[32768,128]{1,0:T(8,128)} async-done(((f32[128,128]{1,0:T(8,128)}), f32[32768,128]{1,0:T(8,128)}) %all-gather.3.cloned.1.call-update) | async-done | bytes 16777232 | tf_op jit(solution)/shard_map/all_gather | solution.py:79
  1086.7 6.6 reduce_sum.18
  1093.5 11.7 %cholesky.100 = f32[128,128]{1,0:T(8,128)S(1)} custom-call(f32[128,128]{1,0:T(8,128)S(1)} %fusion.74), custom_call_target="Cholesky" | custom-call | tf_op jit(solution)/shard_map/jit(cholesky)/cholesky | solution.py:91
  1106.5 9.8 custom-call.44
  1118.0 28.6 %psum.23 = f32[]{:T(128)} all-reduce(f32[]{:T(128)} %get-tuple-element.278), channel_id=1, replica_groups=mesh['space'=32,'fac'=8] {'fac'}, use_global_device_ids=true, to_apply=%region_16.17 | all-reduce | flops 1 | bytes 8 | tf_op jit(solution)/shard_map/psum | solution.py:97
  (145 shorter events, 42.8 us)
Async XLA Ops:
  8.0 6.4 copy-start
  8.0 6.4 copy-start.1
  8.0 172.1 %reduce-scatter.5.cloned.1.call-start = ((), (), s32[]{:S(2)}) async-start(), calls=%async_computation.4 | async-start | bytes 1990656 | tf_op jit(solution)/shard_map/reduce_scatter | solution.py:84
  9.1 5.3 collective-permute-start
  10.4 4.0 collective-permute-start.1
  37.1 1.9 copy-start.6
  43.3 4.4 copy-start.11
  81.5 267.0 %reduce-scatter.3.cloned.1.call-start = ((), (), s32[]{:S(2)}) async-start(), calls=%async_computation.3 | async-start | bytes 7962624 | tf_op jit(solution)/shard_map/reduce_scatter | solution.py:83
  84.3 2.7 copy-start.2
  85.6 2.7 copy-start.3
  87.0 2.7 copy-start.4
  88.3 2.7 copy-start.5
  92.4 527.3 %all-reduce.7.cloned.1.call-start = ((), (), s32[]{:S(2)}) async-start(), calls=%async_computation.5 | async-start | bytes 2211840 | tf_op jit(solution)/shard_map/psum | solution.py:81
  348.4 2.9 copy-start.10
  348.5 738.2 %all-gather.3.cloned.1.call-start = ((), (), s32[]{:S(2)}) async-start(), calls=%async_computation.2 | async-start | bytes 16842752 | tf_op jit(solution)/shard_map/all_gather | solution.py:79
  619.8 1.7 copy-start.7
  621.6 11.8 %copy-start.8 = (f32[432,432]{1,0:T(8,128)}, f32[432,432]{1,0:T(8,128)S(1)}, u32[]{:S(2)}) copy-start(f32[432,432]{1,0:T(8,128)S(1)} %fusion.25) | copy-start | bytes 2239492
  645.8 55.6 %copy-start.12 = (f32[128,80]{1,0:T(8,128)S(1)}, f32[128,80]{1,0:T(8,128)}, u32[]{:S(2)}) copy-start(f32[128,80]{1,0:T(8,128)} %pad_convert_fusion) | copy-start | bytes 122884
  657.9 43.6 %copy-start.13 = (f32[3,128,128]{2,1,0:T(8,128)S(1)}, f32[3,128,128]{2,1,0:T(8,128)}, u32[]{:S(2)}) copy-start(f32[3,128,128]{2,1,0:T(8,128)} %custom-call.51) | copy-start | bytes 589828
  691.0 56.0 %copy-start.9 = (f32[1,432,128]{2,1,0:T(8,128)S(1)}, f32[1,432,128]{2,1,0:T(8,128)}, u32[]{:S(2)}) copy-start(f32[1,432,128]{2,1,0:T(8,128)} %get-tuple-element.19) | copy-start | bytes 663556
Sparse Core Ops, SparseCore 0:
  81.6 98.4 reduce-scatter.4
  184.4 163.9 reduce-scatter.2
  351.4 268.3 all-reduce.6
Sparse Core Ops, SparseCore 1:
  350.8 735.8 all-gather.2
